TPU v7x, 256 devices: a whole 4x4x8 slice. The times are simulated.
256 devices in a mesh: ctx: 8 (over y, core), tp: 8 (over z), vocab: 4 (over x).
Axes of the slice: x: 4, y: 4, z: 8, core: 2. Of those that a mesh axis runs over, the one named last changes fastest.
Arguments:
- lengths: int32 [8], replicated, may hold values from 4096 to 16384, as said below
- queries: bfloat16 [8, 16384], P(None, 'tp'), may hold values from -15 to 15
- cache_keys: bfloat16 [8, 16384, 1024], P(None, ('ctx', 'vocab'), 'tp'), may hold values from -6 to 6
- cache_values: bfloat16 [8, 16384, 1024], P(None, ('ctx', 'vocab'), 'tp'), may hold values from -6 to 6
- out_weight: bfloat16 [16384, 16384], P('tp', ('ctx', 'vocab')), may hold values from -0.09375 to 0.09375
- residual: bfloat16 [8, 16384], P(None, ('ctx', 'vocab')), may hold values from -6 to 6
- norm_gain: float32 [16384], P(('ctx', 'vocab')), may hold values from 0.5 to 1.5
- head_weight: bfloat16 [16384, 65536], P(('ctx', 'vocab'), 'tp'), may hold values from -0.25 to 0.25
Outputs:
- log_probs: float32 [8, 65536], P(None, 'tp')
Inputs may be any that keep to these rules, and one draw needn't show every extreme that they name: `lengths`: in every draw one row has length exactly 16384.
All inputs are finite; a program needn't handle non-finite values.
Results may differ from a plain program's by a relative error of at most 0.0025.
Values sent between devices are 32-bit elements; how exact they have to be, the bound alone decides.
A program may use at most 64 MiB of HBM per device.

v0:
```python
import jax
import jax.numpy as jnp
from jax import lax
from jax.sharding import PartitionSpec as P

D = 16384
HD = 128


def joined(part, axis, combine):
    gathered = jax.tree.map(lambda a: lax.all_gather(a, axis), part)

    def take(source):
        return jax.tree.map(lambda a: lax.dynamic_index_in_dim(a, source, 0, False), gathered)

    return lax.fori_loop(
        1, lax.axis_size(axis), lambda source, state: combine(state, take(source)), take(0)
    )


def attend_block(queries, cache_keys, cache_values, lengths, first_slot):
    row_count = queries.shape[0]
    kv_local = cache_keys.shape[2] // HD
    group_size = queries.shape[1] // cache_keys.shape[2]
    slot_count = cache_keys.shape[1]
    query_heads = queries.reshape(row_count, kv_local, group_size, HD)
    key_heads = cache_keys.reshape(row_count, slot_count, kv_local, HD)
    value_heads = cache_values.reshape(row_count, slot_count, kv_local, HD)
    scores = jnp.einsum(
        "bkgd,bckd->bkgc", query_heads, key_heads, preferred_element_type=jnp.float32
    ) * HD ** (-0.5)
    position = first_slot + jnp.arange(slot_count, dtype=jnp.int32)
    valid = (position[None, :] < lengths[:, None])[:, None, None, :]
    masked = jnp.where(valid, scores, -1e30)
    local_peak = jnp.max(masked, axis=3)
    expo = jnp.where(valid, jnp.exp(masked - local_peak[..., None]), 0.0)
    totals = jnp.sum(expo, axis=3)
    mixed = jnp.einsum(
        "bkgc,bckd->bkgd",
        expo.astype(jnp.bfloat16),
        value_heads,
        preferred_element_type=jnp.float32,
    )
    return (local_peak, totals, mixed)


def combine_stats(first_part, second_part):
    peak_value = jnp.maximum(first_part[0], second_part[0])
    totals = first_part[1] * jnp.exp(first_part[0] - peak_value) + second_part[1] * jnp.exp(
        second_part[0] - peak_value
    )
    return (peak_value, totals)


def local_stats(logits):
    peak_logit = jnp.max(logits, axis=1)
    return (peak_logit, jnp.sum(jnp.exp(logits - peak_logit[:, None]), axis=1))


def shards(
    lengths, queries, cache_keys, cache_values, out_weight, residual, norm_gain, head_weight
):
    first_slot = lax.axis_index(("ctx", "vocab")) * cache_keys.shape[1]
    local_peak, totals, mixed = attend_block(queries, cache_keys, cache_values, lengths, first_slot)
    peak_value = lax.pmax(local_peak, ("ctx", "vocab"))
    factor = jnp.exp(local_peak - peak_value)
    totals, mixed = lax.psum((totals * factor, mixed * factor[..., None]), ("ctx", "vocab"))
    attended = (
        (mixed / totals[..., None]).astype(jnp.bfloat16).reshape(queries.shape[0], queries.shape[1])
    )
    partial_out = jnp.dot(attended, out_weight, preferred_element_type=jnp.float32)
    hidden = residual.astype(jnp.float32) + lax.psum(partial_out, "tp")
    square_sum = lax.psum(jnp.sum(hidden * hidden, axis=1), ("ctx", "vocab"))
    normed = (hidden * lax.rsqrt(square_sum / D + 1e-05)[:, None] * norm_gain).astype(jnp.bfloat16)
    head_terms = jnp.dot(normed, head_weight, preferred_element_type=jnp.float32)
    logits = lax.psum(head_terms, ("ctx", "vocab"))
    peak_logit, exp_total = joined(local_stats(logits), "tp", combine_stats)
    return logits - peak_logit[:, None] - jnp.log(exp_total)[:, None]


def solution(mesh):
    return jax.shard_map(
        shards,
        mesh=mesh,
        in_specs=(
            P(),
            P(None, "tp"),
            P(None, ("ctx", "vocab"), "tp"),
            P(None, ("ctx", "vocab"), "tp"),
            P("tp", ("ctx", "vocab")),
            P(None, ("ctx", "vocab")),
            P(("ctx", "vocab")),
            P(("ctx", "vocab"), "tp"),
        ),
        out_specs=P(None, "tp"),
        check_vma=False,
    )
```

profile of v0, /device:TPU:1, one launch (start us, length us, event | category | flops | bytes accessed | tf_op | source)
XLA Modules:
  0.0 416.7 jit_solution(6949711031054165341)
XLA Ops:
  6.5 0.9 broadcast_compare_fusion
  7.4 1.7 fusion.21
  9.1 0.2 fusion.4
  9.3 64.1 %pmax.7 = f32[8,1,16]{2,0,1:T(8,128)S(1)} all-reduce(f32[8,1,16]{2,0,1:T(8,128)S(1)} %bitcast.42), channel_id=1, replica_groups=mesh['ctx'=8,'tp'=8,'vocab'=4] {'ctx','vocab'}, use_global_device_ids=true, to_apply=%region_1.2 | all-reduce | flops 128 | bytes 1024 | tf_op jit(solution)/shard_map/pmax | solution.py:65
  73.5 2.2 fusion.3
  75.7 62.4 %psum.36 = f32[8,16]{1,0:T(8,128)S(1)} all-reduce(f32[8,16]{1,0:T(8,128)S(1)} %get-tuple-element.154), channel_id=1, replica_groups=mesh['ctx'=8,'tp'=8,'vocab'=4] {'ctx','vocab'}, use_global_device_ids=true, to_apply=%region_4.5 | all-reduce | flops 128 | bytes 1024 | tf_op jit(solution)/shard_map/psum | solution.py:67
  138.1 45.8 %all-reduce.6.cloned.1.call-done = f32[8,1,16,128]{3,2,0,1:T(8,128)} async-done(((f32[8,1,16,128]{3,2,0,1:T(8,128)}), f32[8,1,16,128]{3,2,0,1:T(8,128)}) %all-reduce.6.cloned.1.call-update) | async-done | bytes 65552 | tf_op jit(solution)/shard_map/psum | solution.py:67
  183.9 0.9 fusion.14
  184.8 0.4 fusion.10
  185.2 23.4 %psum.37 = f32[8,512]{1,0:T(8,128)S(1)} all-reduce(f32[8,512]{1,0:T(8,128)S(1)} %fusion.10), channel_id=1, replica_groups=mesh['ctx'=8,'tp'=8,'vocab'=4] {'tp'}, use_global_device_ids=true, to_apply=%region_5.6 | all-reduce | flops 4096 | bytes 32768 | tf_op jit(solution)/shard_map/psum | solution.py:72
  208.6 0.8 multiply_reduce_fusion
  209.4 65.6 %psum.38 = f32[8]{0:T(128)S(1)} all-reduce(f32[8]{0:T(128)S(1)} %multiply_reduce_fusion), channel_id=1, replica_groups=mesh['ctx'=8,'tp'=8,'vocab'=4] {'ctx','vocab'}, use_global_device_ids=true, to_apply=%region_7.8 | all-reduce | flops 8 | bytes 64 | tf_op jit(solution)/shard_map/psum | solution.py:73
  275.0 5.4 %fusion.15 = f32[8,8192]{1,0:T(8,128)} fusion(bf16[512,8192]{1,0:T(8,128)(2,1)} %param.17, f32[8,512]{1,0:T(8,128)S(1)} %psum.37, bf16[8,512]{1,0:T(8,128)(2,1)} %param.15, f32[512]{0:T(512)} %param.16, f32[8]{0:T(128)S(1)} %add_rsqrt_fusion), kind=kOutput, calls=%fused_computation.27 | convolution fusion | flops 67129344 | bytes 8677408 | tf_op jit(solution)/shard_map/dot_general | solution.py:75
  280.4 0.6 dynamic-slice
  281.7 109.4 %all-reduce.8.cloned.1.call-done = f32[8,8192]{1,0:T(8,128)} async-done(((f32[8,8192]{1,0:T(8,128)}), f32[8,8192]{1,0:T(8,128)}) %all-reduce.8.cloned.1.call-update) | async-done | bytes 262160 | tf_op jit(solution)/shard_map/psum | solution.py:76
  391.1 1.1 reduce_max.22
  392.2 0.2 dynamic-update-slice
  392.5 1.2 exponential_reduce_fusion
  393.7 0.2 dynamic-update-slice.1
  393.9 13.7 %all-reduce.2 = (f32[64]{0:T(128)S(1)}, f32[64]{0:T(128)S(1)}) all-reduce(f32[64]{0:T(128)S(1)} %dynamic-update-slice, f32[64]{0:T(128)S(1)} %dynamic-update-slice.1), channel_id=2, replica_groups=mesh['ctx'=8,'tp'=8,'vocab'=4] {'tp'}, use_global_device_ids=true, to_apply=%add | all-reduce | flops 128 | bytes 1024
  407.6 0.1 reshape.73
  407.7 0.1 reshape.74
  407.8 0.3 while.17
  408.1 1.7 subtract_subtract_fusion
  (21 shorter events, 0.3 us)
Async XLA Ops:
  6.5 178.3 %copy-start = (bf16[2048,512]{1,0:T(8,128)(2,1)S(1)}, bf16[2048,512]{1,0:T(8,128)(2,1)}, u32[]{:S(2)}) copy-start(bf16[2048,512]{1,0:T(8,128)(2,1)} %param.14) | copy-start | bytes 6291460
  6.5 177.4 %all-reduce.6.cloned.1.call-start = ((), (), s32[]{:S(2)}) async-start(), calls=%async_computation | async-start | bytes 131072 | tf_op jit(solution)/shard_map/psum | solution.py:67
  73.5 206.9 %copy-start.1 = (u32[256]{0:T(256)S(1)}, u32[256]{0:T(256)}, u32[]{:S(2)}) copy-start(u32[256]{0:T(256)} %constant.76) | copy-start | bytes 3076
  75.7 315.4 %all-reduce.8.cloned.1.call-start = ((), (), s32[]{:S(2)}) async-start(), calls=%async_computation.1 | async-start | bytes 524288 | tf_op jit(solution)/shard_map/psum | solution.py:76
Sparse Core Ops, SparseCore 0:
  75.8 108.0 all-reduce.5
  280.5 110.5 all-reduce.7
where the time goes:
time: 421 us; the launch traced here: 417 us
  blocking collectives  229 us (54%)
  waiting for transfers between devices  155 us (37%)
  between operations  14.1 us (3%)
  matrix products  9.62 us (2%)
  other arithmetic  7.1 us (2%)
    psum x1, waiting for transfers between devices, shards(): logits = lax.psum(head_terms, ('ctx', 'vocab'))  109 us
    psum x1, blocking collectives, shards(): square_sum = lax.psum(jnp.sum(hidden * hidden, axis=1), ('ctx', 'vocab'))  65.6 us
    pmax x1, blocking collectives, shards(): peak_value = lax.pmax(local_peak, ('ctx', 'vocab'))  64.1 us
    psum x1, blocking collectives, shards(): lax.psum((totals * factor, mixed * factor[..., None]), ('ctx', 'vocab'))  62.4 us
    psum x1, waiting for transfers between devices, shards(): lax.psum((totals * factor, mixed * factor[..., None]), ('ctx', 'vocab'))  45.8 us
    psum x1, blocking collectives, shards(): hidden = residual.astype(jnp.float32) + lax.psum(partial_out, 'tp')  23.4 us
    unnamed x1, blocking collectives  13.7 us
  transfers between devices with their start and end apart: 2, of which 2 were waited for; matrix products, arithmetic and copies ran while one was open for 0% of the time, Pallas kernels for 0%

commit v1 on v0

v1 whole, which is shorter than its diff:
```python
import functools

import jax
import jax.numpy as jnp
from jax import lax
from jax.experimental import pallas as pl
from jax.experimental.pallas import tpu as pltpu
from jax.sharding import PartitionSpec as P

MESH = pl.DeviceIdType.MESH
B = 8
D = 16384
HD = 128
GROUP = 16
CTX, TP, VOCAB = 8, 8, 4
PLANE = CTX * VOCAB
SLOTS = 512
FEAT = 512
VSLICE = 256
F32 = jnp.float32
BF16 = jnp.bfloat16


def kernel(
    len_hbm, q_hbm, k_hbm, v_hbm, w_hbm, res_hbm, gain_hbm, head_hbm,
    out_ref,
    lens, q, k, v, w, res, gain, head, qs,
    part, parts, att, proj, terms, gathered, fin, zstat, pstat,
    load_sem, send_sem, recv_sem,
):
    ctx, tp, voc = lax.axis_index("ctx"), lax.axis_index("tp"), lax.axis_index("vocab")
    me = ctx * VOCAB + voc

    loads = [
        pltpu.make_async_copy(src, dst, load_sem.at[i])
        for i, (src, dst) in enumerate(
            [(q_hbm, q), (len_hbm, lens), (k_hbm, k), (v_hbm, v), (w_hbm, w), (res_hbm, res), (gain_hbm, gain), (head_hbm, head)]
        )
    ]
    for load in loads:
        load.start()

    def plane_peer(step):
        c = lax.rem(ctx + step // VOCAB, CTX)
        x = lax.rem(voc + lax.rem(step, VOCAB), VOCAB)
        return c * VOCAB + x, (c, tp, x)

    def z_peer(step):
        return (ctx, lax.rem(tp + step, TP), voc)

    barrier = pltpu.get_barrier_semaphore()

    def greet_plane(step, carry):
        pl.semaphore_signal(barrier, inc=1, device_id=plane_peer(step)[1], device_id_type=MESH)
        return carry

    def greet_z(step, carry):
        pl.semaphore_signal(barrier, inc=1, device_id=z_peer(step), device_id_type=MESH)
        return carry

    lax.fori_loop(1, PLANE, greet_plane, 0)
    lax.fori_loop(1, TP, greet_z, 0)

    def send(stage, src, dst, device):
        pltpu.make_async_remote_copy(
            src_ref=src, dst_ref=dst, send_sem=send_sem.at[stage], recv_sem=recv_sem.at[stage],
            device_id=device, device_id_type=MESH,
        ).start()

    def await_bytes(sem, like):
        pltpu.make_async_copy(like, like, sem).wait()

    loads[0].wait()
    for h in range(GROUP):
        qs[pl.ds(h * B, B), :] = q[:, h * HD : (h + 1) * HD].astype(F32)
    loads[1].wait()
    loads[2].wait()
    loads[3].wait()
    position = me * SLOTS + lax.broadcasted_iota(jnp.int32, (GROUP, SLOTS), 1)
    lane = lax.broadcasted_iota(jnp.int32, (GROUP, HD), 1)
    for b in range(B):
        query = qs[pl.ds(b, GROUP, stride=B), :].astype(BF16)
        scores = lax.dot_general(query, k[b], (((1,), (1,)), ((), ())), preferred_element_type=F32) * HD ** (-0.5)
        valid = position < lens[b]
        masked = jnp.where(valid, scores, -1e30)
        peak = jnp.max(masked, axis=1, keepdims=True)
        expo = jnp.where(valid, jnp.exp(masked - peak), 0.0)
        total = jnp.sum(expo, axis=1, keepdims=True)
        mixed = jnp.dot(expo.astype(BF16), v[b], preferred_element_type=F32)
        row = (b // 4) * 8 + b % 4
        part[pl.ds(row, GROUP, stride=16), :] = mixed
        part[pl.ds(row + 4, GROUP, stride=16), :] = jnp.where(lane < 64, peak, total)

    pl.semaphore_wait(barrier, PLANE - 1 + TP - 1)

    def scatter_part(step, carry):
        slot, device = plane_peer(step)
        send(0, part.at[pl.ds(pl.multiple_of(slot * 8, 8), 8), :], parts.at[me], device)
        return carry

    lax.fori_loop(1, PLANE, scatter_part, 0)
    parts[me] = part[pl.ds(pl.multiple_of(me * 8, 8), 8), :]
    await_bytes(recv_sem.at[0], parts.at[pl.ds(0, PLANE - 1)])
    stats = parts[:, 4:8, :]
    swapped = pltpu.roll(stats.reshape(PLANE * 4, HD), 64, 1).reshape(PLANE, 4, HD)
    low = lax.broadcasted_iota(jnp.int32, (PLANE, 4, HD), 2) < 64
    peaks = jnp.where(low, stats, swapped)
    totals = jnp.where(low, swapped, stats)
    top = jnp.max(peaks, axis=0, keepdims=True)
    factor = jnp.exp(peaks - top)
    total = jnp.sum(totals * factor, axis=0)
    attended = jnp.sum(parts[:, 0:4, :] * factor, axis=0) / total
    att[me] = attended

    def gather_att(step, carry):
        send(1, att.at[me], att.at[me], plane_peer(step)[1])
        return carry

    lax.fori_loop(1, PLANE, gather_att, 0)
    loads[4].wait()
    await_bytes(recv_sem.at[1], att.at[pl.ds(0, PLANE - 1)])
    heads = [
        jnp.concatenate([att[2 * h], att[2 * h + 1]], axis=0).astype(BF16) for h in range(GROUP)
    ]
    proj[tp] = jnp.dot(jnp.concatenate(heads, axis=1), w[...], preferred_element_type=F32)

    def gather_proj(step, carry):
        send(2, proj.at[tp], proj.at[tp], z_peer(step))
        return carry

    lax.fori_loop(1, TP, gather_proj, 0)
    loads[5].wait()
    loads[6].wait()
    loads[7].wait()
    await_bytes(recv_sem.at[2], proj.at[pl.ds(0, TP - 1)])
    hidden = res[...].astype(F32) + jnp.sum(proj[...], axis=0)
    diagonal = lax.broadcasted_iota(jnp.int32, (B, HD), 0) == lax.broadcasted_iota(jnp.int32, (B, HD), 1)
    squares = jnp.sum(hidden * hidden, axis=1, keepdims=True)
    square_row = jnp.sum(jnp.where(diagonal, squares, 0.0), axis=0, keepdims=True)
    scaled = (hidden * gain[...].reshape(1, FEAT)).astype(BF16)

    def head_block(step, carry):
        c = lax.rem(ctx + step, CTX)
        width = VOCAB * VSLICE
        columns = pl.ds(pl.multiple_of(c * width, width), width)
        block = jnp.dot(scaled, head[:, columns], preferred_element_type=F32)
        for x in range(VOCAB):
            slot = c * VOCAB + x
            terms[slot, 0:8, :] = block[:, x * VSLICE : x * VSLICE + HD]
            terms[slot, 8:16, :] = block[:, x * VSLICE + HD : (x + 1) * VSLICE]
            terms[slot, 16:17, :] = square_row

            @pl.when(slot != me)
            def _():
                send(3, terms.at[slot, pl.ds(0, 17)], gathered.at[me, pl.ds(0, 17)], (c, tp, x))

        return carry

    lax.fori_loop(0, CTX, head_block, 0)
    gathered[me, 0:17, :] = terms[me, 0:17, :]
    await_bytes(recv_sem.at[3], gathered.at[pl.ds(0, PLANE - 1), pl.ds(0, 17)])
    summed = jnp.sum(gathered[:, 0:16, :], axis=0)
    square_sum = jnp.sum(jnp.where(diagonal, jnp.sum(gathered[:, 16:17, :], axis=0), 0.0), axis=1, keepdims=True)
    logits = jnp.concatenate([summed[0:8], summed[8:16]], axis=1) * lax.rsqrt(square_sum / D + 1e-05)
    mine = pl.ds(pl.multiple_of(me * VSLICE, VSLICE), VSLICE)
    fin[:, mine] = logits

    def gather_logits(step, carry):
        send(4, fin.at[:, mine], fin.at[:, mine], plane_peer(step)[1])
        return carry

    half = lax.broadcasted_iota(jnp.int32, (B, HD), 1) < 64

    def merge(pairs):
        turned = pltpu.roll(pairs.reshape(-1, HD), 64, 1).reshape(pairs.shape)
        low = lax.broadcasted_iota(jnp.int32, pairs.shape, 2) < 64
        tops = jnp.where(low, pairs, turned)
        sums = jnp.where(low, turned, pairs)
        top = jnp.max(tops, axis=0)
        return top, jnp.sum(sums * jnp.exp(tops - top[None]), axis=0)

    top = jnp.max(logits, axis=1, keepdims=True)
    total = jnp.sum(jnp.exp(logits - top), axis=1, keepdims=True)
    zstat[tp] = jnp.where(half, top, total)

    def gather_zstat(step, carry):
        send(5, zstat.at[tp], zstat.at[tp], z_peer(step))
        return carry

    lax.fori_loop(1, TP, gather_zstat, 0)
    lax.fori_loop(1, PLANE, gather_logits, 0)
    await_bytes(recv_sem.at[5], zstat.at[pl.ds(0, TP - 1)])
    pstat[me] = jnp.where(half, *merge(zstat[...]))

    def gather_pstat(step, carry):
        send(6, pstat.at[me], pstat.at[me], plane_peer(step)[1])
        return carry

    lax.fori_loop(1, PLANE, gather_pstat, 0)
    await_bytes(recv_sem.at[6], pstat.at[pl.ds(0, PLANE - 1)])
    top, total = merge(pstat[...])
    shift = (top + jnp.log(total))[:, 0:1]
    await_bytes(recv_sem.at[4], fin.at[:, pl.ds(0, (PLANE - 1) * VSLICE)])
    out_ref[...] = fin[...] - shift

    await_bytes(send_sem.at[0], parts.at[pl.ds(0, PLANE - 1)])
    await_bytes(send_sem.at[1], att.at[pl.ds(0, PLANE - 1)])
    await_bytes(send_sem.at[2], proj.at[pl.ds(0, TP - 1)])
    await_bytes(send_sem.at[3], gathered.at[pl.ds(0, PLANE - 1), pl.ds(0, 17)])
    await_bytes(send_sem.at[4], fin.at[:, pl.ds(0, (PLANE - 1) * VSLICE)])
    await_bytes(send_sem.at[5], zstat.at[pl.ds(0, TP - 1)])
    await_bytes(send_sem.at[6], pstat.at[pl.ds(0, PLANE - 1)])


def shards(*args):
    vmem = pltpu.VMEM
    width = PLANE * VSLICE
    return pl.pallas_call(
        kernel,
        out_shape=jax.ShapeDtypeStruct((B, width), F32),
        in_specs=[pl.BlockSpec(memory_space=pl.ANY)] * 8,
        out_specs=pl.BlockSpec(memory_space=vmem),
        scratch_shapes=[
            pltpu.SMEM((B,), jnp.int32),
            vmem((B, GROUP * HD), BF16),
            vmem((B, SLOTS, HD), BF16),
            vmem((B, SLOTS, HD), BF16),
            vmem((GROUP * HD, FEAT), BF16),
            vmem((B, FEAT), BF16),
            vmem((FEAT,), F32),
            vmem((FEAT, width), BF16),
            vmem((GROUP * B, HD), F32),
            vmem((PLANE * 8, HD), F32),
            vmem((PLANE, 8, HD), F32),
            vmem((PLANE, 4, HD), F32),
            vmem((TP, B, FEAT), F32),
            vmem((PLANE, 24, HD), F32),
            vmem((PLANE, 24, HD), F32),
            vmem((B, width), F32),
            vmem((TP, B, HD), F32),
            vmem((PLANE, B, HD), F32),
            pltpu.SemaphoreType.DMA((8,)),
            pltpu.SemaphoreType.DMA((7,)),
            pltpu.SemaphoreType.DMA((7,)),
        ],
        compiler_params=pltpu.CompilerParams(
            collective_id=0, has_side_effects=True, vmem_limit_bytes=40 * 1024 * 1024
        ),
    )(*args)


def solution(mesh):
    return jax.shard_map(
        shards,
        mesh=mesh,
        in_specs=(
            P(),
            P(None, "tp"),
            P(None, ("ctx", "vocab"), "tp"),
            P(None, ("ctx", "vocab"), "tp"),
            P("tp", ("ctx", "vocab")),
            P(None, ("ctx", "vocab")),
            P(("ctx", "vocab")),
            P(("ctx", "vocab"), "tp"),
        ),
        out_specs=P(None, "tp"),
        check_vma=False,
    )
```

time: 421 us -> 56.7 us (0.13)
  blocking collectives: 229 us -> 0 us
  waiting for transfers between devices: 155 us -> 0 us
  Pallas kernels: 0 us -> 45.4 us
  between operations: 14.1 us -> 0.02 us
  local copies, waits for them, and re-layouts: 1.26 us -> 10.9 us
  matrix products: 9.62 us -> 0 us
  other arithmetic: 7.1 us -> 0 us
    psum x2 -> x0, waiting for transfers between devices: 155 us -> none  [the longest x1 109 us: shards(): logits = lax.psum(head_terms, ('ctx', 'vocab'))]
    psum x3 -> x0, blocking collectives: 151 us -> none  [the longest x1 65.6 us: shards(): square_sum = lax.psum(jnp.sum(hidden * hidden, axis=1), ('ctx', 'vocab'))]
    pmax x1 -> x0, blocking collectives: 64.1 us -> none  [shards(): peak_value = lax.pmax(local_peak, ('ctx', 'vocab'))]
    pallas_call x0 -> x1, Pallas kernels: none -> 45.4 us  [shards(): pl.pallas_call(kernel, out_shape=jax.ShapeDtypeStruct((B, width), F32), i...]
    unnamed x1 -> x0, blocking collectives: 13.7 us -> none
    unnamed x9 -> x17, local copies, waits for them, and re-layouts: 1.1 us -> 10.9 us
    dot_general x4 -> x0, matrix products: 9.62 us -> none  [the longest x1 5.35 us: shards(): jnp.dot(normed, head_weight, preferred_element_type=jnp.float32)]
  transfers between devices with their start and end apart: 2 -> 0, of which waited for: 2 -> 0; matrix products, arithmetic and copies ran while one was open for 0% -> 0% of each run, Pallas kernels for 0% -> 0%
where the time goes in v1:
time: 56.7 us; the launch traced here: 56.3 us
  Pallas kernels  45.4 us (80%)
  local copies, waits for them, and re-layouts  10.9 us (19%)
    pallas_call x1, Pallas kernels, shards(): pl.pallas_call(kernel, out_shape=jax.ShapeDtypeStruct((B, width), F32), i...  45.4 us
    unnamed x17, local copies, waits for them, and re-layouts  10.9 us

profile of v1, /device:TPU:1, one launch (start us, length us, event | category | flops | bytes accessed | tf_op | source)
XLA Modules:
  0.0 56.3 jit_solution(14185412619333192558)
XLA Ops:
  0.0 0.0 copy-start
  0.0 3.4 %copy-done = bf16[512,8192]{1,0:T(8,128)(2,1)S(1)} copy-done((bf16[512,8192]{1,0:T(8,128)(2,1)S(1)}, bf16[512,8192]{1,0:T(8,128)(2,1)}, u32[]{:S(2)}) %copy-start) | copy-done | bytes 8388632
  3.4 0.0 copy-start.1
  3.4 1.6 %copy-done.1 = bf16[2048,512]{1,0:T(8,128)(2,1)S(1)} copy-done((bf16[2048,512]{1,0:T(8,128)(2,1)S(1)}, bf16[2048,512]{1,0:T(8,128)(2,1)}, u32[]{:S(2)}) %copy-start.1) | copy-done | bytes 2097176
  5.0 0.0 copy-start.2
  5.0 1.2 %copy-done.2 = bf16[8,512,128]{2,1,0:T(8,128)(2,1)S(1)} copy-done((bf16[8,512,128]{2,1,0:T(8,128)(2,1)S(1)}, bf16[8,512,128]{2,1,0:T(8,128)(2,1)}, u32[]{:S(2)}) %copy-start.2) | copy-done | bytes 1048600
  6.2 0.0 copy-start.3
  6.2 1.2 %copy-done.3 = bf16[8,512,128]{2,1,0:T(8,128)(2,1)S(1)} copy-done((bf16[8,512,128]{2,1,0:T(8,128)(2,1)S(1)}, bf16[8,512,128]{2,1,0:T(8,128)(2,1)}, u32[]{:S(2)}) %copy-start.3) | copy-done | bytes 1048600
  7.4 0.0 copy-start.4
  7.4 0.8 %copy-done.4 = bf16[8,2048]{1,0:T(8,128)(2,1)S(1)} copy-done((bf16[8,2048]{1,0:T(8,128)(2,1)S(1)}, bf16[8,2048]{1,0:T(8,128)(2,1)}, u32[]{:S(2)}) %copy-start.4) | copy-done | bytes 32792
  8.2 0.0 copy-start.5
  8.2 0.7 %copy-done.5 = bf16[8,512]{1,0:T(8,128)(2,1)S(1)} copy-done((bf16[8,512]{1,0:T(8,128)(2,1)S(1)}, bf16[8,512]{1,0:T(8,128)(2,1)}, u32[]{:S(2)}) %copy-start.5) | copy-done | bytes 8216
  8.9 0.0 copy-start.6
  8.9 0.7 %copy-done.6 = f32[512]{0:T(512)S(1)} copy-done((f32[512]{0:T(512)S(1)}, f32[512]{0:T(512)}, u32[]{:S(2)}) %copy-start.6) | copy-done | bytes 2072
  9.6 0.0 copy-start.7
  9.6 0.7 %copy-done.7 = s32[8]{0:T(128)S(1)} copy-done((s32[8]{0:T(128)S(1)}, s32[8]{0:T(128)}, u32[]{:S(2)}) %copy-start.7) | copy-done | bytes 56
  10.2 45.4 %shard_map.82 = f32[8,8192]{1,0:T(8,128)S(1)} custom-call(s32[8]{0:T(128)S(1)} %copy-done.7, bf16[8,2048]{1,0:T(8,128)(2,1)S(1)} %copy-done.4, bf16[8,512,128]{2,1,0:T(8,128)(2,1)S(1)} %copy-done.2, bf16[8,512,128]{2,1,0:T(8,128)(2,1)S(1)} %copy-done.3, bf16[2048,512]{1,0:T(8,128)(2,1)S(1)} %copy-done.1, bf16[8,512]{1,0:T(8,128)(2,1)S(1)} %copy-done.5, ...), custom_call_target="tpu_custom_call" | custom-call | tf_op jit(solution)/shard_map/pallas_call | solution.py:218
  55.6 0.7 %copy.10 = f32[8,8192]{1,0:T(8,128)} copy(f32[8,8192]{1,0:T(8,128)S(1)} %shard_map.82) | data formatting | bytes 524288
Async XLA Ops:
  0.0 3.4 %copy-start = (bf16[512,8192]{1,0:T(8,128)(2,1)S(1)}, bf16[512,8192]{1,0:T(8,128)(2,1)}, u32[]{:S(2)}) copy-start(bf16[512,8192]{1,0:T(8,128)(2,1)} %head_hbm.1) | copy-start | bytes 25165828
  3.4 1.6 %copy-start.1 = (bf16[2048,512]{1,0:T(8,128)(2,1)S(1)}, bf16[2048,512]{1,0:T(8,128)(2,1)}, u32[]{:S(2)}) copy-start(bf16[2048,512]{1,0:T(8,128)(2,1)} %w_hbm.1) | copy-start | bytes 6291460
  5.0 1.2 %copy-start.2 = (bf16[8,512,128]{2,1,0:T(8,128)(2,1)S(1)}, bf16[8,512,128]{2,1,0:T(8,128)(2,1)}, u32[]{:S(2)}) copy-start(bf16[8,512,128]{2,1,0:T(8,128)(2,1)} %k_hbm.1) | copy-start | bytes 3145732
  6.2 1.2 %copy-start.3 = (bf16[8,512,128]{2,1,0:T(8,128)(2,1)S(1)}, bf16[8,512,128]{2,1,0:T(8,128)(2,1)}, u32[]{:S(2)}) copy-start(bf16[8,512,128]{2,1,0:T(8,128)(2,1)} %v_hbm.1) | copy-start | bytes 3145732
  7.4 0.8 %copy-start.4 = (bf16[8,2048]{1,0:T(8,128)(2,1)S(1)}, bf16[8,2048]{1,0:T(8,128)(2,1)}, u32[]{:S(2)}) copy-start(bf16[8,2048]{1,0:T(8,128)(2,1)} %q_hbm.1) | copy-start | bytes 98308
  8.2 0.7 %copy-start.5 = (bf16[8,512]{1,0:T(8,128)(2,1)S(1)}, bf16[8,512]{1,0:T(8,128)(2,1)}, u32[]{:S(2)}) copy-start(bf16[8,512]{1,0:T(8,128)(2,1)} %res_hbm.1) | copy-start | bytes 24580
  8.9 0.7 %copy-start.6 = (f32[512]{0:T(512)S(1)}, f32[512]{0:T(512)}, u32[]{:S(2)}) copy-start(f32[512]{0:T(512)} %gain_hbm.1) | copy-start | bytes 6148
  9.6 0.7 %copy-start.7 = (s32[8]{0:T(128)S(1)}, s32[8]{0:T(128)}, u32[]{:S(2)}) copy-start(s32[8]{0:T(128)} %len_hbm.1) | copy-start | bytes 100

commit v2 on v1

v2 whole, which is shorter than its diff:
```python
import functools

import jax
import jax.numpy as jnp
from jax import lax
from jax.experimental import pallas as pl
from jax.experimental.pallas import tpu as pltpu
from jax.sharding import PartitionSpec as P

MESH = pl.DeviceIdType.MESH
CHIPS = sorted(((dy, dx) for dy in range(4) for dx in range(4)), key=lambda d: -(min(d[0], 4 - d[0]) + min(d[1], 4 - d[1])))
Z_STEPS = (4, 3, 5, 2, 6, 1, 7)
B = 8
D = 16384
HD = 128
GROUP = 16
CTX, TP, VOCAB = 8, 8, 4
PLANE = CTX * VOCAB
SLOTS = 512
FEAT = 512
VSLICE = 256
F32 = jnp.float32
BF16 = jnp.bfloat16

def kernel(
    len_hbm, q_hbm, k_hbm, v_hbm, w_hbm, res_hbm, gain_hbm, head_hbm,
    out_ref,
    lens, q, k, v, w, res, gain, head, qs,
    part, parts, att, proj, terms, gathered, fin, allstat,
    load_sem, send_sem, recv_sem,
):
    ctx, tp, voc = lax.axis_index("ctx"), lax.axis_index("tp"), lax.axis_index("vocab")
    me = ctx * VOCAB + voc

    chip_y, core = ctx // 2, lax.rem(ctx, 2)
    rows = [lax.rem(chip_y + d, 4) for d in range(4)]
    columns = [lax.rem(voc + d, 4) for d in range(4)]
    cores = [core, 1 - core]
    chips = [(rows[dy], columns[dx]) for dy, dx in CHIPS]
    plane = [
        ((y * 2 + c) * VOCAB + x, (y * 2 + c, tp, x))
        for (y, x), offset in zip(chips, CHIPS)
        for c in reversed(cores)
        if offset != (0, 0) or c is not core
    ]
    line = [(ctx, lax.rem(tp + d, TP), voc) for d in Z_STEPS]

    barrier = pltpu.get_barrier_semaphore()
    for device in line + [device for _, device in plane]:
        pl.semaphore_signal(barrier, inc=1, device_id=device, device_id_type=MESH)

    loads = [
        pltpu.make_async_copy(src, dst, load_sem.at[i])
        for i, (src, dst) in enumerate(
            [(q_hbm, q), (len_hbm, lens), (k_hbm, k), (v_hbm, v), (w_hbm, w), (res_hbm, res), (gain_hbm, gain), (head_hbm, head)]
        )
    ]
    for load in loads:
        load.start()

    def send(stage, src, dst, device):
        pltpu.make_async_remote_copy(
            src_ref=src, dst_ref=dst, send_sem=send_sem.at[stage], recv_sem=recv_sem.at[stage],
            device_id=device, device_id_type=MESH,
        ).start()

    def await_bytes(sem, like):
        pltpu.make_async_copy(like, like, sem).wait()

    loads[0].wait()
    for h in range(GROUP):
        qs[pl.ds(h * B, B), :] = q[:, h * HD : (h + 1) * HD].astype(F32)
    loads[1].wait()
    loads[2].wait()
    loads[3].wait()
    position = me * SLOTS + lax.broadcasted_iota(jnp.int32, (GROUP, SLOTS), 1)
    lane = lax.broadcasted_iota(jnp.int32, (GROUP, HD), 1)
    for b in range(B):
        query = qs[pl.ds(b, GROUP, stride=B), :].astype(BF16)
        scores = lax.dot_general(query, k[b], (((1,), (1,)), ((), ())), preferred_element_type=F32) * HD ** (-0.5)
        valid = position < lens[b]
        masked = jnp.where(valid, scores, -1e30)
        peak = jnp.max(masked, axis=1, keepdims=True)
        expo = jnp.where(valid, jnp.exp(masked - peak), 0.0)
        total = jnp.sum(expo, axis=1, keepdims=True)
        mixed = jnp.dot(expo.astype(BF16), v[b], preferred_element_type=F32)
        row = (b // 4) * 8 + b % 4
        part[pl.ds(row, GROUP, stride=16), :] = mixed
        part[pl.ds(row + 4, GROUP, stride=16), :] = jnp.where(lane < 64, peak, total)

    pl.semaphore_wait(barrier, PLANE - 1 + TP - 1)

    for slot, device in plane:
        send(0, part.at[pl.ds(pl.multiple_of(slot * 8, 8), 8), :], parts.at[me], device)
    parts[me] = part[pl.ds(pl.multiple_of(me * 8, 8), 8), :]
    await_bytes(recv_sem.at[0], parts.at[pl.ds(0, PLANE - 1)])

    stats = parts[:, 4:8, :]
    swapped = pltpu.roll(stats.reshape(PLANE * 4, HD), 64, 1).reshape(PLANE, 4, HD)
    low = lax.broadcasted_iota(jnp.int32, (PLANE, 4, HD), 2) < 64
    peaks = jnp.where(low, stats, swapped)
    totals = jnp.where(low, swapped, stats)
    top = jnp.max(peaks, axis=0, keepdims=True)
    factor = jnp.exp(peaks - top)
    total = jnp.sum(totals * factor, axis=0)
    attended = jnp.sum(parts[:, 0:4, :] * factor, axis=0) / total
    att[me] = attended

    for _, device in plane:
        send(1, att.at[me], att.at[me], device)
    loads[4].wait()
    await_bytes(recv_sem.at[1], att.at[pl.ds(0, PLANE - 1)])

    heads = [
        jnp.concatenate([att[2 * h], att[2 * h + 1]], axis=0).astype(BF16) for h in range(GROUP)
    ]
    proj[tp] = jnp.dot(jnp.concatenate(heads, axis=1), w[...], preferred_element_type=F32)

    for device in line:
        send(2, proj.at[tp], proj.at[tp], device)
    loads[5].wait()
    loads[6].wait()
    loads[7].wait()
    await_bytes(recv_sem.at[2], proj.at[pl.ds(0, TP - 1)])

    hidden = res[...].astype(F32) + jnp.sum(proj[...], axis=0)
    diagonal = lax.broadcasted_iota(jnp.int32, (B, HD), 0) == lax.broadcasted_iota(jnp.int32, (B, HD), 1)
    squares = jnp.sum(hidden * hidden, axis=1, keepdims=True)
    square_row = jnp.sum(jnp.where(diagonal, squares, 0.0), axis=0, keepdims=True)
    scaled = (hidden * gain[...].reshape(1, FEAT)).astype(BF16)

    for (y, x), offset in zip(chips, CHIPS):
        pair = y * VOCAB + x
        width = 2 * VSLICE
        block = jnp.dot(scaled, head[:, pl.ds(pl.multiple_of(pair * width, width), width)], preferred_element_type=F32)
        for c in range(2):
            slot = pair * 2 + c
            terms[slot, 0:8, :] = block[:, c * VSLICE : c * VSLICE + HD]
            terms[slot, 8:16, :] = block[:, c * VSLICE + HD : (c + 1) * VSLICE]
            terms[slot, 16:17, :] = square_row
        for c in reversed(cores):
            if offset != (0, 0) or c is not core:
                send(3, terms.at[pair * 2 + c, pl.ds(0, 17)], gathered.at[me, pl.ds(0, 17)], (y * 2 + c, tp, x))

    slice_index = (chip_y * VOCAB + voc) * 2 + core
    gathered[me, 0:17, :] = terms[slice_index, 0:17, :]

    await_bytes(recv_sem.at[3], gathered.at[pl.ds(0, PLANE - 1), pl.ds(0, 17)])

    summed = jnp.sum(gathered[:, 0:16, :], axis=0)
    square_sum = jnp.sum(jnp.where(diagonal, jnp.sum(gathered[:, 16:17, :], axis=0), 0.0), axis=1, keepdims=True)
    logits = jnp.concatenate([summed[0:8], summed[8:16]], axis=1) * lax.rsqrt(square_sum / D + 1e-05)
    mine = pl.ds(pl.multiple_of(slice_index * VSLICE, VSLICE), VSLICE)
    fin[:, mine] = logits

    paired = lax.rem(lax.broadcasted_iota(jnp.int32, (B, HD), 1), 64) == lax.broadcasted_iota(jnp.int32, (B, HD), 0)
    half = lax.broadcasted_iota(jnp.int32, (B, HD), 1) < 64

    def merge(pairs):
        turned = pltpu.roll(pairs.reshape(-1, HD), 64, 1).reshape(pairs.shape)
        low = lax.broadcasted_iota(jnp.int32, pairs.shape, 2) < 64
        tops = jnp.where(low, pairs, turned)
        sums = jnp.where(low, turned, pairs)
        top = jnp.max(tops, axis=0)
        return top, jnp.sum(sums * jnp.exp(tops - top[None]), axis=0)

    top = jnp.max(logits, axis=1, keepdims=True)
    total = jnp.sum(jnp.exp(logits - top), axis=1, keepdims=True)
    here = me * TP + tp
    allstat[here] = jnp.sum(jnp.where(paired, jnp.where(half, top, total), 0.0), axis=0, keepdims=True)

    def gather_stat(step, carry):
        t = lax.rem(tp + 4 + (1 - 2 * lax.rem(step, 2)) * ((step + 1) // 2), TP)
        for _, (c, _, x) in plane:
            send(5, allstat.at[here], allstat.at[here], (c, t, x))
        return carry
    for _, device in plane:
        send(4, fin.at[:, mine], fin.at[:, mine], device)
    lax.fori_loop(0, 8, gather_stat, 0)
    for t_line in line:
        send(5, allstat.at[here], allstat.at[here], t_line)

    await_bytes(recv_sem.at[5], allstat.at[pl.ds(0, PLANE * TP - 1)])

    pairs = allstat[...]
    best = jnp.max(pairs, axis=0, keepdims=True)
    turned = pltpu.roll(pairs.reshape(PLANE * TP, HD), 64, 1).reshape(pairs.shape)
    sums = jnp.sum(turned * jnp.exp(jnp.minimum(pairs - best, 0.0)), axis=0, keepdims=True)
    shift = jnp.sum(jnp.where(diagonal, (best + jnp.log(sums)).reshape(1, HD), 0.0), axis=1, keepdims=True)
    await_bytes(recv_sem.at[4], fin.at[:, pl.ds(0, (PLANE - 1) * VSLICE)])
    out_ref[...] = fin[...] - shift

    await_bytes(send_sem.at[0], parts.at[pl.ds(0, PLANE - 1)])
    await_bytes(send_sem.at[1], att.at[pl.ds(0, PLANE - 1)])
    await_bytes(send_sem.at[2], proj.at[pl.ds(0, TP - 1)])
    await_bytes(send_sem.at[3], gathered.at[pl.ds(0, PLANE - 1), pl.ds(0, 17)])
    await_bytes(send_sem.at[4], fin.at[:, pl.ds(0, (PLANE - 1) * VSLICE)])
    await_bytes(send_sem.at[5], allstat.at[pl.ds(0, PLANE * TP - 1)])

def shards(*args):
    vmem = pltpu.VMEM
    width = PLANE * VSLICE
    return pl.pallas_call(
        kernel,
        out_shape=pltpu.VMEM((B, width), F32),
        in_specs=[pl.BlockSpec(memory_space=pl.ANY)] * 8,
        out_specs=pl.BlockSpec(memory_space=vmem),
        scratch_shapes=[
            pltpu.SMEM((B,), jnp.int32),
            vmem((B, GROUP * HD), BF16),
            vmem((B, SLOTS, HD), BF16),
            vmem((B, SLOTS, HD), BF16),
            vmem((GROUP * HD, FEAT), BF16),
            vmem((B, FEAT), BF16),
            vmem((FEAT,), F32),
            vmem((FEAT, width), BF16),
            vmem((GROUP * B, HD), F32),
            vmem((PLANE * 8, HD), F32),
            vmem((PLANE, 8, HD), F32),
            vmem((PLANE, 4, HD), F32),
            vmem((TP, B, FEAT), F32),
            vmem((PLANE, 24, HD), F32),
            vmem((PLANE, 24, HD), F32),
            vmem((B, width), F32),
            vmem((PLANE * TP, 1, HD), F32),
            pltpu.SemaphoreType.DMA((8,)),
            pltpu.SemaphoreType.DMA((7,)),
            pltpu.SemaphoreType.DMA((7,)),
        ],
        compiler_params=pltpu.CompilerParams(
            collective_id=0, has_side_effects=True, vmem_limit_bytes=40 * 1024 * 1024
        ),
    )(*[pltpu.with_memory_space_constraint(a, pltpu.HBM) for a in args])

def solution(mesh):
    return jax.shard_map(
        shards,
        mesh=mesh,
        in_specs=(
            P(),
            P(None, "tp"),
            P(None, ("ctx", "vocab"), "tp"),
            P(None, ("ctx", "vocab"), "tp"),
            P("tp", ("ctx", "vocab")),
            P(None, ("ctx", "vocab")),
            P(("ctx", "vocab")),
            P(("ctx", "vocab"), "tp"),
        ),
        out_specs=P(None, "tp"),
        check_vma=False,
    )
```

time: 56.7 us -> 42.3 us (0.75)
  local copies, waits for them, and re-layouts: 10.9 us -> 0.71 us
  Pallas kernels: 45.4 us -> 41.5 us
    unnamed x17 -> x1, local copies, waits for them, and re-layouts: 10.9 us -> 0.71 us
    pallas_call x1, Pallas kernels: 45.4 us -> 41.5 us  [shards(): pl.pallas_call(kernel, out_shape=pltpu.VMEM((B, width), F32), in_specs=[p...]
where the time goes in v2:
time: 42.3 us; the launch traced here: 42.2 us
  Pallas kernels  41.5 us (98%)
  local copies, waits for them, and re-layouts  0.71 us (2%)
    pallas_call x1, Pallas kernels, shards(): pl.pallas_call(kernel, out_shape=pltpu.VMEM((B, width), F32), in_specs=[p...  41.5 us

profile of v2, /device:TPU:1, one launch (start us, length us, event | category | flops | bytes accessed | tf_op | source)
XLA Modules:
  0.0 42.2 jit_solution(13866588563541487159)
XLA Ops:
  0.0 41.5 %shard_map.82 = f32[8,8192]{1,0:T(8,128)S(1)} custom-call(s32[8]{0:T(128)} %len_hbm.1, bf16[8,2048]{1,0:T(8,128)(2,1)} %q_hbm.1, bf16[8,512,128]{2,1,0:T(8,128)(2,1)} %k_hbm.1, bf16[8,512,128]{2,1,0:T(8,128)(2,1)} %v_hbm.1, bf16[2048,512]{1,0:T(8,128)(2,1)} %w_hbm.1, bf16[8,512]{1,0:T(8,128)(2,1)} %res_hbm.1, f32[512]{0:T(512)} %gain_hbm.1, ...), custom_call_target="tpu_custom_call" | custom-call | tf_op jit(solution)/shard_map/pallas_call | solution.py:203
  41.5 0.7 %copy.10 = f32[8,8192]{1,0:T(8,128)} copy(f32[8,8192]{1,0:T(8,128)S(1)} %shard_map.82) | data formatting | bytes 524288

commit v3 on v2

--- a/solution.py
+++ b/solution.py
@@ -26,7 +26,7 @@
     len_hbm, q_hbm, k_hbm, v_hbm, w_hbm, res_hbm, gain_hbm, head_hbm,
     out_ref,
     lens, q, k, v, w, res, gain, head, qs,
-    part, parts, att, proj, terms, gathered, fin, allstat,
+    part, parts, att, proj, terms, gathered, fin, allstat, rowlike,
     load_sem, send_sem, recv_sem,
 ):
     ctx, tp, voc = lax.axis_index("ctx"), lax.axis_index("tp"), lax.axis_index("vocab")
@@ -46,7 +46,7 @@
     line = [(ctx, lax.rem(tp + d, TP), voc) for d in Z_STEPS]
 
     barrier = pltpu.get_barrier_semaphore()
-    for device in line + [device for _, device in plane]:
+    for device in [device for _, device in plane] + line:
         pl.semaphore_signal(barrier, inc=1, device_id=device, device_id_type=MESH)
 
     loads = [
@@ -72,21 +72,29 @@
         qs[pl.ds(h * B, B), :] = q[:, h * HD : (h + 1) * HD].astype(F32)
     loads[1].wait()
     loads[2].wait()
-    loads[3].wait()
     position = me * SLOTS + lax.broadcasted_iota(jnp.int32, (GROUP, SLOTS), 1)
     lane = lax.broadcasted_iota(jnp.int32, (GROUP, HD), 1)
+    scores = jnp.concatenate(
+        [
+            lax.dot_general(
+                qs[pl.ds(b, GROUP, stride=B), :].astype(BF16), k[b], (((1,), (1,)), ((), ())), preferred_element_type=F32
+            )
+            for b in range(B)
+        ],
+        axis=0,
+    ) * HD ** (-0.5)
+    valid = jnp.concatenate([position < lens[b] for b in range(B)], axis=0)
+    masked = jnp.where(valid, scores, -1e30)
+    peak = jnp.max(masked, axis=1, keepdims=True)
+    expo = jnp.where(valid, jnp.exp(masked - peak), 0.0)
+    total = jnp.sum(expo, axis=1, keepdims=True)
+    weights = expo.astype(BF16)
+    loads[3].wait()
     for b in range(B):
-        query = qs[pl.ds(b, GROUP, stride=B), :].astype(BF16)
-        scores = lax.dot_general(query, k[b], (((1,), (1,)), ((), ())), preferred_element_type=F32) * HD ** (-0.5)
-        valid = position < lens[b]
-        masked = jnp.where(valid, scores, -1e30)
-        peak = jnp.max(masked, axis=1, keepdims=True)
-        expo = jnp.where(valid, jnp.exp(masked - peak), 0.0)
-        total = jnp.sum(expo, axis=1, keepdims=True)
-        mixed = jnp.dot(expo.astype(BF16), v[b], preferred_element_type=F32)
-        row = (b // 4) * 8 + b % 4
-        part[pl.ds(row, GROUP, stride=16), :] = mixed
-        part[pl.ds(row + 4, GROUP, stride=16), :] = jnp.where(lane < 64, peak, total)
+        mine = slice(b * GROUP, (b + 1) * GROUP)
+        at = (b // 4) * 8 + b % 4
+        part[pl.ds(at, GROUP, stride=16), :] = jnp.dot(weights[mine], v[b], preferred_element_type=F32)
+        part[pl.ds(at + 4, GROUP, stride=16), :] = jnp.where(lane < 64, peak[mine], total[mine])
 
     pl.semaphore_wait(barrier, PLANE - 1 + TP - 1)
 
@@ -129,18 +137,30 @@
     square_row = jnp.sum(jnp.where(diagonal, squares, 0.0), axis=0, keepdims=True)
     scaled = (hidden * gain[...].reshape(1, FEAT)).astype(BF16)
 
-    for (y, x), offset in zip(chips, CHIPS):
-        pair = y * VOCAB + x
+    def head_terms(y, x):
         width = 2 * VSLICE
-        block = jnp.dot(scaled, head[:, pl.ds(pl.multiple_of(pair * width, width), width)], preferred_element_type=F32)
+        columns = pl.ds(pl.multiple_of((y * VOCAB + x) * width, width), width)
+        return jnp.dot(scaled, head[:, columns], preferred_element_type=F32)
+
+    def send_terms(block, y, x, offset):
         for c in range(2):
-            slot = pair * 2 + c
+            slot = (y * VOCAB + x) * 2 + c
             terms[slot, 0:8, :] = block[:, c * VSLICE : c * VSLICE + HD]
             terms[slot, 8:16, :] = block[:, c * VSLICE + HD : (c + 1) * VSLICE]
             terms[slot, 16:17, :] = square_row
         for c in reversed(cores):
             if offset != (0, 0) or c is not core:
-                send(3, terms.at[pair * 2 + c, pl.ds(0, 17)], gathered.at[me, pl.ds(0, 17)], (y * 2 + c, tp, x))
+                slot = (y * VOCAB + x) * 2 + c
+                send(3, terms.at[slot, pl.ds(0, 17)], gathered.at[me, pl.ds(0, 17)], (y * 2 + c, tp, x))
+
+    ahead = []
+    for (y, x), offset in zip(chips, CHIPS):
+        ahead.append((head_terms(y, x), y, x, offset))
+        if len(ahead) > 2:
+            for _ in range(1):
+                send_terms(*ahead.pop(0))
+    for block in ahead:
+        send_terms(*block)
 
     slice_index = (chip_y * VOCAB + voc) * 2 + core
     gathered[me, 0:17, :] = terms[slice_index, 0:17, :]
@@ -153,39 +173,26 @@
     mine = pl.ds(pl.multiple_of(slice_index * VSLICE, VSLICE), VSLICE)
     fin[:, mine] = logits
 
-    paired = lax.rem(lax.broadcasted_iota(jnp.int32, (B, HD), 1), 64) == lax.broadcasted_iota(jnp.int32, (B, HD), 0)
-    half = lax.broadcasted_iota(jnp.int32, (B, HD), 1) < 64
-
-    def merge(pairs):
-        turned = pltpu.roll(pairs.reshape(-1, HD), 64, 1).reshape(pairs.shape)
-        low = lax.broadcasted_iota(jnp.int32, pairs.shape, 2) < 64
-        tops = jnp.where(low, pairs, turned)
-        sums = jnp.where(low, turned, pairs)
-        top = jnp.max(tops, axis=0)
-        return top, jnp.sum(sums * jnp.exp(tops - top[None]), axis=0)
-
     top = jnp.max(logits, axis=1, keepdims=True)
-    total = jnp.sum(jnp.exp(logits - top), axis=1, keepdims=True)
-    here = me * TP + tp
-    allstat[here] = jnp.sum(jnp.where(paired, jnp.where(half, top, total), 0.0), axis=0, keepdims=True)
+    local = top + jnp.log(jnp.sum(jnp.exp(logits - top), axis=1, keepdims=True))
+    allstat[me, pl.ds(tp, 1), :] = jnp.sum(jnp.where(diagonal, local, 0.0), axis=0, keepdims=True)
 
     def gather_stat(step, carry):
         t = lax.rem(tp + 4 + (1 - 2 * lax.rem(step, 2)) * ((step + 1) // 2), TP)
         for _, (c, _, x) in plane:
-            send(5, allstat.at[here], allstat.at[here], (c, t, x))
+            send(5, allstat.at[me, pl.ds(tp, 1), :], allstat.at[me, pl.ds(tp, 1), :], (c, t, x))
         return carry
     for _, device in plane:
         send(4, fin.at[:, mine], fin.at[:, mine], device)
     lax.fori_loop(0, 8, gather_stat, 0)
     for t_line in line:
-        send(5, allstat.at[here], allstat.at[here], t_line)
-
-    await_bytes(recv_sem.at[5], allstat.at[pl.ds(0, PLANE * TP - 1)])
-
-    pairs = allstat[...]
-    best = jnp.max(pairs, axis=0, keepdims=True)
-    turned = pltpu.roll(pairs.reshape(PLANE * TP, HD), 64, 1).reshape(pairs.shape)
-    sums = jnp.sum(turned * jnp.exp(jnp.minimum(pairs - best, 0.0)), axis=0, keepdims=True)
+        send(5, allstat.at[me, pl.ds(tp, 1), :], allstat.at[me, pl.ds(tp, 1), :], t_line)
+
+    await_bytes(recv_sem.at[5], rowlike.at[pl.ds(0, PLANE * TP - 1)])
+
+    slices = allstat[...]
+    best = jnp.max(jnp.max(slices, axis=0), axis=0, keepdims=True)
+    sums = jnp.sum(jnp.sum(jnp.exp(slices - best[None]), axis=0), axis=0, keepdims=True)
     shift = jnp.sum(jnp.where(diagonal, (best + jnp.log(sums)).reshape(1, HD), 0.0), axis=1, keepdims=True)
     await_bytes(recv_sem.at[4], fin.at[:, pl.ds(0, (PLANE - 1) * VSLICE)])
     out_ref[...] = fin[...] - shift
@@ -195,7 +202,7 @@
     await_bytes(send_sem.at[2], proj.at[pl.ds(0, TP - 1)])
     await_bytes(send_sem.at[3], gathered.at[pl.ds(0, PLANE - 1), pl.ds(0, 17)])
     await_bytes(send_sem.at[4], fin.at[:, pl.ds(0, (PLANE - 1) * VSLICE)])
-    await_bytes(send_sem.at[5], allstat.at[pl.ds(0, PLANE * TP - 1)])
+    await_bytes(send_sem.at[5], rowlike.at[pl.ds(0, PLANE * TP - 1)])
 
 def shards(*args):
     vmem = pltpu.VMEM
@@ -222,6 +229,7 @@
             vmem((PLANE, 24, HD), F32),
             vmem((PLANE, 24, HD), F32),
             vmem((B, width), F32),
+            vmem((PLANE, TP, HD), F32),
             vmem((PLANE * TP, 1, HD), F32),
             pltpu.SemaphoreType.DMA((8,)),
             pltpu.SemaphoreType.DMA((7,)),

time: 42.3 us -> 40.7 us (0.962)
  Pallas kernels: 41.5 us -> 39.9 us
    pallas_call x1, Pallas kernels: 41.5 us -> 39.9 us  [shards(): pl.pallas_call(kernel, out_shape=pltpu.VMEM((B, width), F32), in_specs=[p...]
where the time goes in v3:
time: 40.7 us; the launch traced here: 40.6 us
  Pallas kernels  39.9 us (98%)
  local copies, waits for them, and re-layouts  0.71 us (2%)
    pallas_call x1, Pallas kernels, shards(): pl.pallas_call(kernel, out_shape=pltpu.VMEM((B, width), F32), in_specs=[p...  39.9 us

profile of v3, /device:TPU:1, one launch (start us, length us, event | category | flops | bytes accessed | tf_op | source)
XLA Modules:
  0.0 40.6 jit_solution(13222571404358483920)
XLA Ops:
  0.0 39.9 %shard_map.82 = f32[8,8192]{1,0:T(8,128)S(1)} custom-call(s32[8]{0:T(128)} %len_hbm.1, bf16[8,2048]{1,0:T(8,128)(2,1)} %q_hbm.1, bf16[8,512,128]{2,1,0:T(8,128)(2,1)} %k_hbm.1, bf16[8,512,128]{2,1,0:T(8,128)(2,1)} %v_hbm.1, bf16[2048,512]{1,0:T(8,128)(2,1)} %w_hbm.1, bf16[8,512]{1,0:T(8,128)(2,1)} %res_hbm.1, f32[512]{0:T(512)} %gain_hbm.1, ...), custom_call_target="tpu_custom_call" | custom-call | tf_op jit(solution)/shard_map/pallas_call | solution.py:210
  39.9 0.7 %copy.10 = f32[8,8192]{1,0:T(8,128)} copy(f32[8,8192]{1,0:T(8,128)S(1)} %shard_map.82) | data formatting | bytes 524288

commit v4 on v3

--- a/solution.py
+++ b/solution.py
@@ -30,15 +30,15 @@
     load_sem, send_sem, recv_sem,
 ):
     ctx, tp, voc = lax.axis_index("ctx"), lax.axis_index("tp"), lax.axis_index("vocab")
-    me = ctx * VOCAB + voc
 
     chip_y, core = ctx // 2, lax.rem(ctx, 2)
     rows = [lax.rem(chip_y + d, 4) for d in range(4)]
     columns = [lax.rem(voc + d, 4) for d in range(4)]
     cores = [core, 1 - core]
+    me = (chip_y * VOCAB + voc) * 2 + core
     chips = [(rows[dy], columns[dx]) for dy, dx in CHIPS]
     plane = [
-        ((y * 2 + c) * VOCAB + x, (y * 2 + c, tp, x))
+        ((y * VOCAB + x) * 2 + c, (y * 2 + c, tp, x))
         for (y, x), offset in zip(chips, CHIPS)
         for c in reversed(cores)
         if offset != (0, 0) or c is not core
@@ -72,7 +72,7 @@
         qs[pl.ds(h * B, B), :] = q[:, h * HD : (h + 1) * HD].astype(F32)
     loads[1].wait()
     loads[2].wait()
-    position = me * SLOTS + lax.broadcasted_iota(jnp.int32, (GROUP, SLOTS), 1)
+    position = (ctx * VOCAB + voc) * SLOTS + lax.broadcasted_iota(jnp.int32, (GROUP, SLOTS), 1)
     lane = lax.broadcasted_iota(jnp.int32, (GROUP, HD), 1)
     scores = jnp.concatenate(
         [
@@ -162,16 +162,17 @@
     for block in ahead:
         send_terms(*block)
 
-    slice_index = (chip_y * VOCAB + voc) * 2 + core
-    gathered[me, 0:17, :] = terms[slice_index, 0:17, :]
+    gathered[me, 0:17, :] = terms[me, 0:17, :]
 
     await_bytes(recv_sem.at[3], gathered.at[pl.ds(0, PLANE - 1), pl.ds(0, 17)])
 
     summed = jnp.sum(gathered[:, 0:16, :], axis=0)
     square_sum = jnp.sum(jnp.where(diagonal, jnp.sum(gathered[:, 16:17, :], axis=0), 0.0), axis=1, keepdims=True)
     logits = jnp.concatenate([summed[0:8], summed[8:16]], axis=1) * lax.rsqrt(square_sum / D + 1e-05)
-    mine = pl.ds(pl.multiple_of(slice_index * VSLICE, VSLICE), VSLICE)
+    mine = pl.ds(pl.multiple_of(me * VSLICE, VSLICE), VSLICE)
     fin[:, mine] = logits
+    for _, device in plane:
+        send(4, fin.at[:, mine], fin.at[:, mine], device)
 
     top = jnp.max(logits, axis=1, keepdims=True)
     local = top + jnp.log(jnp.sum(jnp.exp(logits - top), axis=1, keepdims=True))
@@ -182,8 +183,6 @@
         for _, (c, _, x) in plane:
             send(5, allstat.at[me, pl.ds(tp, 1), :], allstat.at[me, pl.ds(tp, 1), :], (c, t, x))
         return carry
-    for _, device in plane:
-        send(4, fin.at[:, mine], fin.at[:, mine], device)
     lax.fori_loop(0, 8, gather_stat, 0)
     for t_line in line:
         send(5, allstat.at[me, pl.ds(tp, 1), :], allstat.at[me, pl.ds(tp, 1), :], t_line)

time: 40.7 us -> 40.5 us (level)
  no operation moved by 1% of the time
where the time goes in v4:
time: 40.5 us; the launch traced here: 40.4 us
  Pallas kernels  39.7 us (98%)
  local copies, waits for them, and re-layouts  0.71 us (2%)
    pallas_call x1, Pallas kernels, shards(): pl.pallas_call(kernel, out_shape=pltpu.VMEM((B, width), F32), in_specs=[p...  39.7 us

profile of v4, /device:TPU:1, one launch (start us, length us, event | category | flops | bytes accessed | tf_op | source)
XLA Modules:
  0.0 40.4 jit_solution(12362182749105456150)
XLA Ops:
  0.0 39.7 %shard_map.82 = f32[8,8192]{1,0:T(8,128)S(1)} custom-call(s32[8]{0:T(128)} %len_hbm.1, bf16[8,2048]{1,0:T(8,128)(2,1)} %q_hbm.1, bf16[8,512,128]{2,1,0:T(8,128)(2,1)} %k_hbm.1, bf16[8,512,128]{2,1,0:T(8,128)(2,1)} %v_hbm.1, bf16[2048,512]{1,0:T(8,128)(2,1)} %w_hbm.1, bf16[8,512]{1,0:T(8,128)(2,1)} %res_hbm.1, f32[512]{0:T(512)} %gain_hbm.1, ...), custom_call_target="tpu_custom_call" | custom-call | tf_op jit(solution)/shard_map/pallas_call | solution.py:209
  39.7 0.7 %copy.10 = f32[8,8192]{1,0:T(8,128)} copy(f32[8,8192]{1,0:T(8,128)S(1)} %shard_map.82) | data formatting | bytes 524288

commit v5 on v4

--- a/solution.py
+++ b/solution.py
@@ -46,7 +46,7 @@
     line = [(ctx, lax.rem(tp + d, TP), voc) for d in Z_STEPS]
 
     barrier = pltpu.get_barrier_semaphore()
-    for device in [device for _, device in plane] + line:
+    for device in line[:3] + [device for _, device in plane] + line[3:]:
         pl.semaphore_signal(barrier, inc=1, device_id=device, device_id_type=MESH)
 
     loads = [
@@ -89,29 +89,32 @@
     expo = jnp.where(valid, jnp.exp(masked - peak), 0.0)
     total = jnp.sum(expo, axis=1, keepdims=True)
     weights = expo.astype(BF16)
+    live = total > 0.0
+    inverse = jnp.where(live, 1.0 / jnp.where(live, total, 1.0), 0.0)
+    level = jnp.where(live, peak + jnp.log(jnp.where(live, total, 1.0)), -1e30)
     loads[3].wait()
     for b in range(B):
         mine = slice(b * GROUP, (b + 1) * GROUP)
         at = (b // 4) * 8 + b % 4
-        part[pl.ds(at, GROUP, stride=16), :] = jnp.dot(weights[mine], v[b], preferred_element_type=F32)
-        part[pl.ds(at + 4, GROUP, stride=16), :] = jnp.where(lane < 64, peak[mine], total[mine])
+        part[pl.ds(at, GROUP, stride=16), :] = jnp.dot(weights[mine], v[b], preferred_element_type=F32) * inverse[mine]
+        if b % 2:
+            before = slice((b - 1) * GROUP, b * GROUP)
+            part[pl.ds((b // 4) * 8 + 4 + (b % 4) // 2, GROUP, stride=16), :] = jnp.where(lane < 64, level[before], level[mine])
 
     pl.semaphore_wait(barrier, PLANE - 1 + TP - 1)
 
     for slot, device in plane:
-        send(0, part.at[pl.ds(pl.multiple_of(slot * 8, 8), 8), :], parts.at[me], device)
+        send(0, part.at[pl.ds(pl.multiple_of(slot * 8, 8), 6), :], parts.at[me, pl.ds(0, 6)], device)
     parts[me] = part[pl.ds(pl.multiple_of(me * 8, 8), 8), :]
-    await_bytes(recv_sem.at[0], parts.at[pl.ds(0, PLANE - 1)])
-
-    stats = parts[:, 4:8, :]
-    swapped = pltpu.roll(stats.reshape(PLANE * 4, HD), 64, 1).reshape(PLANE, 4, HD)
+    await_bytes(recv_sem.at[0], parts.at[pl.ds(0, PLANE - 1), pl.ds(0, 6)])
+
+    first = lax.broadcasted_iota(jnp.int32, (PLANE, 4, HD), 1)
+    pairs = jnp.where(first < 2, parts[:, 4:5, :], parts[:, 5:6, :])
+    turned = pltpu.roll(pairs.reshape(PLANE * 4, HD), 64, 1).reshape(PLANE, 4, HD)
     low = lax.broadcasted_iota(jnp.int32, (PLANE, 4, HD), 2) < 64
-    peaks = jnp.where(low, stats, swapped)
-    totals = jnp.where(low, swapped, stats)
-    top = jnp.max(peaks, axis=0, keepdims=True)
-    factor = jnp.exp(peaks - top)
-    total = jnp.sum(totals * factor, axis=0)
-    attended = jnp.sum(parts[:, 0:4, :] * factor, axis=0) / total
+    levels = jnp.where(low == (lax.rem(first, 2) == 0), pairs, turned)
+    factor = jnp.exp(levels - jnp.max(levels, axis=0, keepdims=True))
+    attended = jnp.sum(parts[:, 0:4, :] * factor, axis=0) / jnp.sum(factor, axis=0)
     att[me] = attended
 
     for _, device in plane:
@@ -196,7 +199,7 @@
     await_bytes(recv_sem.at[4], fin.at[:, pl.ds(0, (PLANE - 1) * VSLICE)])
     out_ref[...] = fin[...] - shift
 
-    await_bytes(send_sem.at[0], parts.at[pl.ds(0, PLANE - 1)])
+    await_bytes(send_sem.at[0], parts.at[pl.ds(0, PLANE - 1), pl.ds(0, 6)])
     await_bytes(send_sem.at[1], att.at[pl.ds(0, PLANE - 1)])
     await_bytes(send_sem.at[2], proj.at[pl.ds(0, TP - 1)])
     await_bytes(send_sem.at[3], gathered.at[pl.ds(0, PLANE - 1), pl.ds(0, 17)])
@@ -220,8 +223,8 @@
             vmem((B, FEAT), BF16),
             vmem((FEAT,), F32),
             vmem((FEAT, width), BF16),
-            vmem((GROUP * B, HD), F32),
-            vmem((PLANE * 8, HD), F32),
+            vmem((GROUP * B + B, HD), F32),
+            vmem((PLANE * 8 + 16, HD), F32),
             vmem((PLANE, 8, HD), F32),
             vmem((PLANE, 4, HD), F32),
             vmem((TP, B, FEAT), F32),

time: 40.5 us -> 40.4 us (level)
  no operation moved by 1% of the time
where the time goes in v5:
time: 40.4 us; the launch traced here: 40.3 us
  Pallas kernels  39.6 us (98%)
  local copies, waits for them, and re-layouts  0.71 us (2%)
    pallas_call x1, Pallas kernels, shards(): pl.pallas_call(kernel, out_shape=pltpu.VMEM((B, width), F32), in_specs=[p...  39.6 us

profile of v5, /device:TPU:1, one launch (start us, length us, event | category | flops | bytes accessed | tf_op | source)
XLA Modules:
  0.0 40.3 jit_solution(14880494878555611209)
XLA Ops:
  0.0 39.6 %shard_map.82 = f32[8,8192]{1,0:T(8,128)S(1)} custom-call(s32[8]{0:T(128)} %len_hbm.1, bf16[8,2048]{1,0:T(8,128)(2,1)} %q_hbm.1, bf16[8,512,128]{2,1,0:T(8,128)(2,1)} %k_hbm.1, bf16[8,512,128]{2,1,0:T(8,128)(2,1)} %v_hbm.1, bf16[2048,512]{1,0:T(8,128)(2,1)} %w_hbm.1, bf16[8,512]{1,0:T(8,128)(2,1)} %res_hbm.1, f32[512]{0:T(512)} %gain_hbm.1, ...), custom_call_target="tpu_custom_call" | custom-call | tf_op jit(solution)/shard_map/pallas_call | solution.py:212
  39.6 0.7 %copy.10 = f32[8,8192]{1,0:T(8,128)} copy(f32[8,8192]{1,0:T(8,128)S(1)} %shard_map.82) | data formatting | bytes 524288

commit v6 on v5

--- a/solution.py
+++ b/solution.py
@@ -40,7 +40,7 @@
     plane = [
         ((y * VOCAB + x) * 2 + c, (y * 2 + c, tp, x))
         for (y, x), offset in zip(chips, CHIPS)
-        for c in reversed(cores)
+        for c in cores
         if offset != (0, 0) or c is not core
     ]
     line = [(ctx, lax.rem(tp + d, TP), voc) for d in Z_STEPS]
@@ -151,7 +151,7 @@
             terms[slot, 0:8, :] = block[:, c * VSLICE : c * VSLICE + HD]
             terms[slot, 8:16, :] = block[:, c * VSLICE + HD : (c + 1) * VSLICE]
             terms[slot, 16:17, :] = square_row
-        for c in reversed(cores):
+        for c in cores:
             if offset != (0, 0) or c is not core:
                 slot = (y * VOCAB + x) * 2 + c
                 send(3, terms.at[slot, pl.ds(0, 17)], gathered.at[me, pl.ds(0, 17)], (y * 2 + c, tp, x))

time: 40.4 us -> 40.6 us (level)
  no operation moved by 1% of the time
where the time goes in v6:
time: 40.6 us; the launch traced here: 40.5 us
  Pallas kernels  39.8 us (98%)
  local copies, waits for them, and re-layouts  0.71 us (2%)
    pallas_call x1, Pallas kernels, shards(): pl.pallas_call(kernel, out_shape=pltpu.VMEM((B, width), F32), in_specs=[p...  39.8 us

profile of v6, /device:TPU:1, one launch (start us, length us, event | category | flops | bytes accessed | tf_op | source)
XLA Modules:
  0.0 40.5 jit_solution(12127366536002878441)
XLA Ops:
  0.0 39.8 %shard_map.82 = f32[8,8192]{1,0:T(8,128)S(1)} custom-call(s32[8]{0:T(128)} %len_hbm.1, bf16[8,2048]{1,0:T(8,128)(2,1)} %q_hbm.1, bf16[8,512,128]{2,1,0:T(8,128)(2,1)} %k_hbm.1, bf16[8,512,128]{2,1,0:T(8,128)(2,1)} %v_hbm.1, bf16[2048,512]{1,0:T(8,128)(2,1)} %w_hbm.1, bf16[8,512]{1,0:T(8,128)(2,1)} %res_hbm.1, f32[512]{0:T(512)} %gain_hbm.1, ...), custom_call_target="tpu_custom_call" | custom-call | tf_op jit(solution)/shard_map/pallas_call | solution.py:212
  39.8 0.7 %copy.10 = f32[8,8192]{1,0:T(8,128)} copy(f32[8,8192]{1,0:T(8,128)S(1)} %shard_map.82) | data formatting | bytes 524288
